TPU v7x, 32 devices: a whole 2x2x4 slice. The times are simulated.
32 devices in a mesh: dp: 8 (over z, y), mp: 4 (over x, core).
Axes of the slice: x: 2, y: 2, z: 4, core: 2. Of those that a mesh axis runs over, the one named last changes fastest.
Arguments:
- tokens: bfloat16 [1536, 1152], P('dp'), may hold values from -6 to 6
- doc_lengths: int32 [16, 2], P('dp'), may hold values from 1 to 48, as said below
- cotangent: bfloat16 [1536, 1152], P('dp'), may hold values from -6 to 6
- query_weight: bfloat16 [1152, 1024], P('dp', 'mp'), may hold values from -0.1875 to 0.1875
- key_weight: bfloat16 [1152, 256], P('dp'), may hold values from -0.1875 to 0.1875
- value_weight: bfloat16 [1152, 256], P('dp'), may hold values from -0.1875 to 0.1875
- out_weight: bfloat16 [1024, 1152], P('mp', 'dp'), may hold values from -0.1875 to 0.1875
- gate_weight: bfloat16 [1152, 6912], P('dp', 'mp'), may hold values from -0.1875 to 0.1875
- up_weight: bfloat16 [1152, 6912], P('dp', 'mp'), may hold values from -0.1875 to 0.1875
- down_weight: bfloat16 [6912, 1152], P('mp', 'dp'), may hold values from -0.078125 to 0.078125
- pre_attn_gain: bfloat16 [1152], P('dp'), may hold values from 0.5 to 1.5
- post_attn_gain: bfloat16 [1152], P('dp'), may hold values from 0.5 to 1.5
- pre_ffn_gain: bfloat16 [1152], P('dp'), may hold values from 0.5 to 1.5
- post_ffn_gain: bfloat16 [1152], P('dp'), may hold values from 0.5 to 1.5
- query_gain: bfloat16 [256], P('dp'), may hold values from 0.5 to 1.5
- key_gain: bfloat16 [256], P('dp'), may hold values from 0.5 to 1.5
Outputs:
- mixed: bfloat16 [1536, 1152], P('dp')
- tokens_grad: float32 [1536, 1152], P('dp')
- query_grad: float32 [1152, 1024], P('dp', 'mp')
- key_grad: float32 [1152, 256], P('dp')
- value_grad: float32 [1152, 256], P('dp')
- out_grad: float32 [1024, 1152], P('mp', 'dp')
- gate_grad: float32 [1152, 6912], P('dp', 'mp')
- up_grad: float32 [1152, 6912], P('dp', 'mp')
- down_grad: float32 [6912, 1152], P('mp', 'dp')
- pre_attn_grad: float32 [1152], P('dp')
- post_attn_grad: float32 [1152], P('dp')
- pre_ffn_grad: float32 [1152], P('dp')
- post_ffn_grad: float32 [1152], P('dp')
- query_gain_grad: float32 [256], P('dp')
- key_gain_grad: float32 [256], P('dp')
Inputs may be any that keep to these rules, and one draw needn't show every extreme that they name: Row b of doc_lengths gives the 2 document lengths of buffer b, the buffers of one index of dp being 2 consecutive rows; the documents lie end to end from the buffer's first row, and the rows after them are padding.
All inputs are finite; a program needn't handle non-finite values.
Results may differ from a plain program's by a relative error of at most 0.019.
Values may be sent and summed in bfloat16 or wider, within the bound.
A program may use at most 128 MiB of HBM per device.

v0:
```python
import jax
import jax.numpy as jnp
from jax import lax
from jax.sharding import PartitionSpec as P

WINDOW = 512
EPSILON = 1e-06
THETA_BASE = 10000.0
NEGATIVE = -1e30


def matmul(left_op, right_op):
    return jnp.dot(left_op, right_op, preferred_element_type=jnp.float32)


def inner_rows(left_op, right_op):
    return lax.dot_general(
        left_op, right_op, (((0,), (0,)), ((), ())), preferred_element_type=jnp.float32
    )


def inner_cols(left_op, right_op):
    return lax.dot_general(
        left_op, right_op, (((1,), (1,)), ((), ())), preferred_element_type=jnp.float32
    )


def normed(values, factor):
    return values * lax.rsqrt(jnp.mean(values * values, axis=-1, keepdims=True) + EPSILON) * factor


def rotate(values, cosine, sine_table):
    half_width = values.shape[-1] // 2
    leading = values[..., :half_width]
    trailing = values[..., half_width:]
    return jnp.concatenate(
        [leading * cosine - trailing * sine_table, trailing * cosine + leading * sine_table],
        axis=-1,
    )


def layout(lengths, row_count):
    batches, docs = lengths.shape
    total = batches * row_count
    index = jnp.arange(total, dtype=jnp.int32)
    buffer = index // row_count
    inside = index % row_count
    order = jnp.arange(docs, dtype=jnp.int32)
    ends = jnp.sum(
        jnp.where(order[None, :, None] >= order[None, None, :], lengths[:, None, :], 0), axis=2
    )
    row_ends = jnp.repeat(ends, row_count, axis=0)
    row_lengths = jnp.repeat(lengths, row_count, axis=0)
    passed = inside[:, None] >= row_ends
    segment = jnp.sum(passed.astype(jnp.int32), axis=1)
    begins = jnp.sum(jnp.where(passed, row_lengths, 0), axis=1)
    position = inside - begins
    live_rows = (segment < docs).astype(jnp.float32)
    group = buffer * (docs + 1) + segment
    allowed = (
        (group[:, None] == group[None, :])
        & (index[None, :] <= index[:, None])
        & (index[:, None] - index[None, :] < WINDOW)
    )
    return (position, live_rows, allowed)


def angles(position, head_width):
    half_width = head_width // 2
    frequency = THETA_BASE ** (-2.0 * jnp.arange(half_width, dtype=jnp.float32) / head_width)
    turned = position.astype(jnp.float32)[:, None] * frequency[None, :]
    return (jnp.cos(turned), jnp.sin(turned))


def on_device(
    tokens,
    doc_lengths,
    cotangent,
    query_weight,
    key_weight,
    value_weight,
    out_weight,
    gate_weight,
    up_weight,
    down_weight,
    pre_attn_gain,
    post_attn_gain,
    pre_ffn_gain,
    post_ffn_gain,
    query_gain,
    key_gain,
):
    low = jnp.bfloat16
    full = jnp.float32
    dp = lax.axis_size("dp")
    mp = lax.axis_size("mp")
    shard = lax.axis_index("mp")
    rows, width = tokens.shape
    share = width // dp
    head_width = query_weight.shape[1]
    units = gate_weight.shape[1] // dp
    own_rows = rows // mp
    own = (shard * own_rows, own_rows)
    gain_head = query_gain.shape[0]
    gains = jnp.concatenate(
        [pre_attn_gain, post_attn_gain, pre_ffn_gain, post_ffn_gain, query_gain, key_gain]
    )
    block = jnp.concatenate([query_weight, key_weight, value_weight, out_weight.T], axis=1)
    gains_row = jnp.pad(gains, (0, block.shape[1] - gains.shape[0]))[None]
    packed = jnp.concatenate([block, jnp.pad(gains_row, ((0, 15), (0, 0)))], axis=0)
    packed = lax.all_gather(packed, "dp", axis=0, tiled=False)
    attn_w = packed[:, :share].reshape(width, 4 * head_width)
    qkv_w = attn_w[:, : 3 * head_width]
    out_wt = attn_w[:, 3 * head_width :]
    all_gains = packed[:, share].astype(full)
    gain_one, gain_two, gain_three, gain_four = (
        all_gains[:, i * share : (i + 1) * share].reshape(width) for i in range(4)
    )
    query_g = all_gains[:, 4 * share : 4 * share + gain_head].reshape(head_width)
    key_g = all_gains[:, 4 * share + gain_head : 4 * share + 2 * gain_head].reshape(head_width)
    ffn_block = jnp.stack([gate_weight, up_weight, down_weight.T], axis=0)
    ffn_block = ffn_block.reshape(3, share, dp, units).transpose(2, 1, 0, 3)
    ffn_block = ffn_block.reshape(dp, share, 3 * units)
    ffn_w = lax.all_to_all(ffn_block, "dp", split_axis=0, concat_axis=0, tiled=True)
    ffn_w = ffn_w.reshape(width, 3 * units)
    glu_w = ffn_w[:, : 2 * units]
    down_wt = ffn_w[:, 2 * units :]
    inputs = tokens.astype(full)
    position, live_rows, allowed = layout(doc_lengths, rows // doc_lengths.shape[0])
    cosine, sine_table = angles(position, head_width)
    normed_in = normed(inputs, gain_one).astype(low)
    projected = matmul(normed_in, qkv_w)
    query_pre = projected[:, :head_width]
    key_pre = projected[:, head_width : 2 * head_width]
    value_low = projected[:, 2 * head_width :].astype(low)
    query_low = rotate(normed(query_pre, query_g), cosine, sine_table).astype(low)
    key_low = rotate(normed(key_pre, key_g), cosine, sine_table).astype(low)
    score_scale = head_width ** (-0.5)
    scores = inner_cols(query_low, key_low) * score_scale
    scores = jnp.where(allowed, scores, NEGATIVE)
    row_peak = jnp.max(scores, axis=1, keepdims=True)
    raised = jnp.exp(scores - row_peak)
    attention = raised / jnp.sum(raised, axis=1, keepdims=True)
    attention_low = attention.astype(low)
    attended = matmul(attention_low, value_low).astype(low)
    attn_part = inner_cols(attended, out_wt).astype(low)
    attn_sum = lax.psum_scatter(attn_part, "mp", scatter_dimension=0, tiled=True).astype(full)
    inputs_own = lax.dynamic_slice_in_dim(tokens, *own, axis=0).astype(full)
    upstream = lax.dynamic_slice_in_dim(cotangent, *own, axis=0).astype(full)
    live = lax.dynamic_slice_in_dim(live_rows, *own, axis=0)[:, None]

    def post_norm(values, factor):
        return normed(values, factor) * live

    attn_out, back_two = jax.vjp(post_norm, attn_sum, gain_two)
    middle = inputs_own + attn_out
    normed_mid_own, back_three = jax.vjp(normed, middle, gain_three)
    normed_mid = lax.all_gather(normed_mid_own.astype(low), ("dp", "mp"), axis=0, tiled=True)
    glu_pre = matmul(normed_mid, glu_w)
    gate_proj = glu_pre[:, :units]
    up_proj = glu_pre[:, units:]

    def glu(gate_in, up_in):
        return jax.nn.gelu(gate_in, approximate=True) * up_in

    hidden_full, back_glu = jax.vjp(glu, gate_proj, up_proj)
    hidden = hidden_full.astype(low)
    ffn_part = inner_cols(hidden, down_wt).astype(low)
    ffn_sum = lax.psum_scatter(ffn_part, ("dp", "mp"), scatter_dimension=0, tiled=True).astype(full)
    ffn_out, back_four = jax.vjp(post_norm, ffn_sum, gain_four)
    mixed_own = (middle + ffn_out).astype(low)
    d_ffn_own, grad_four = back_four(upstream)
    d_ffn = lax.all_gather(d_ffn_own.astype(low), ("dp", "mp"), axis=0, tiled=True)
    grad_down_t = inner_rows(d_ffn, hidden)
    d_hidden = matmul(d_ffn, down_wt)
    d_gate, d_up = back_glu(d_hidden)
    d_glu = jnp.concatenate([d_gate.astype(low), d_up.astype(low)], axis=1)
    d_mid_part = inner_cols(d_glu, glu_w).astype(low)
    d_mid = lax.psum_scatter(d_mid_part, ("dp", "mp"), scatter_dimension=0, tiled=True).astype(full)
    grad_glu = inner_rows(normed_mid, d_glu)
    ffn_grad = jnp.concatenate([grad_glu, grad_down_t], axis=1).astype(low)
    ffn_grad = ffn_grad.reshape(dp, share, 3 * units)
    ffn_grad = lax.all_to_all(ffn_grad, "dp", split_axis=0, concat_axis=0, tiled=True)
    ffn_grad = ffn_grad.reshape(dp, share, 3, units).transpose(2, 1, 0, 3)
    ffn_grad = ffn_grad.reshape(3, share, dp * units).astype(full)
    d_mid_add, grad_three = back_three(d_mid)
    d_middle = upstream + d_mid_add
    d_attn_own, grad_two = back_two(d_middle)
    d_attn = lax.all_gather(d_attn_own.astype(low), "mp", axis=0, tiled=True)
    grad_out_t = inner_rows(d_attn, attended)
    d_attended = matmul(d_attn, out_wt).astype(low)
    d_value = inner_rows(attention_low, d_attended).astype(low)
    d_probs = inner_cols(d_attended, value_low)
    d_scores = attention * (d_probs - jnp.sum(attention * d_probs, axis=1, keepdims=True))
    d_scores = d_scores.astype(low)
    d_query_rot = matmul(d_scores, key_low) * score_scale
    d_key_rot = inner_rows(d_scores, query_low) * score_scale

    def turned(values, factor):
        return rotate(normed(values, factor), cosine, sine_table)

    _, back_query = jax.vjp(turned, query_pre, query_g)
    d_query_pre, grad_qgain = back_query(d_query_rot)
    _, back_key = jax.vjp(turned, key_pre, key_g)
    d_key_pre, grad_kgain = back_key(d_key_rot)
    d_qkv = jnp.concatenate([d_query_pre.astype(low), d_key_pre.astype(low), d_value], axis=1)
    d_in_part = inner_cols(d_qkv, qkv_w).astype(low)
    d_in = lax.psum_scatter(d_in_part, "mp", scatter_dimension=0, tiled=True).astype(full)
    grad_qkv = inner_rows(normed_in, d_qkv)
    _, back_one = jax.vjp(normed, inputs_own, gain_one)
    d_in_add, grad_one = back_one(d_in)
    tokens_grad_own = d_middle + d_in_add
    pieces = [
        g.reshape(dp, -1)
        for g in (grad_one, grad_two, grad_three, grad_four, grad_qgain, grad_kgain)
    ]
    gains_grad = jnp.concatenate(pieces, axis=1)
    gains_grad = jnp.pad(gains_grad, ((0, 0), (0, 4 * head_width - gains_grad.shape[1])))
    weights_grad = jnp.concatenate([grad_qkv, grad_out_t], axis=1).reshape(
        dp, share, 4 * head_width
    )
    owned = jnp.concatenate(
        [weights_grad, jnp.pad(gains_grad[:, None], ((0, 0), (0, 15), (0, 0)))], axis=1
    ).astype(low)
    owned = lax.psum_scatter(owned, "dp", scatter_dimension=0, tiled=True)[0].astype(full)
    shared = jnp.concatenate(
        [
            owned[:share, head_width : 3 * head_width].reshape(-1),
            owned[share, : 4 * share + 2 * gain_head],
        ]
    )
    shared = lax.psum(shared, "mp")
    kv_grad = shared[: 2 * share * head_width].reshape(share, 2 * head_width)
    gain_out = shared[2 * share * head_width :]
    mixed = lax.all_gather(mixed_own, "mp", axis=0, tiled=True)
    tokens_grad = lax.all_gather(tokens_grad_own.astype(low), "mp", axis=0, tiled=True).astype(full)
    return (
        mixed,
        tokens_grad,
        owned[:share, :head_width],
        kv_grad[:, :head_width],
        kv_grad[:, head_width:],
        owned[:share, 3 * head_width :].T,
        ffn_grad[0],
        ffn_grad[1],
        ffn_grad[2].T,
        gain_out[:share],
        gain_out[share : 2 * share],
        gain_out[2 * share : 3 * share],
        gain_out[3 * share : 4 * share],
        gain_out[4 * share : 4 * share + gain_head],
        gain_out[4 * share + gain_head :],
    )


def solution(mesh):
    placed = (
        P("dp", None),
        P("dp", None),
        P("dp", None),
        P("dp", "mp"),
        P("dp", None),
        P("dp", None),
        P("mp", "dp"),
        P("dp", "mp"),
        P("dp", "mp"),
        P("mp", "dp"),
        P("dp"),
        P("dp"),
        P("dp"),
        P("dp"),
        P("dp"),
        P("dp"),
    )
    return jax.shard_map(
        on_device,
        mesh=mesh,
        in_specs=placed,
        out_specs=(
            P("dp", None),
            P("dp", None),
            P("dp", "mp"),
            P("dp", None),
            P("dp", None),
            P("mp", "dp"),
            P("dp", "mp"),
            P("dp", "mp"),
            P("mp", "dp"),
            P("dp"),
            P("dp"),
            P("dp"),
            P("dp"),
            P("dp"),
            P("dp"),
        ),
        check_vma=False,
    )
```

profile of v0, /device:TPU:0, one launch (start us, length us, event | category | flops | bytes accessed | tf_op | source)
XLA Modules:
  0.0 653.2 jit_solution(11283578642979378089)
XLA Ops:
  7.2 4.1 concatenate.49
  11.3 1.8 fusion.25
  15.0 1.2 fusion.16
  16.2 54.4 %all-gather.9.cloned.1.call-done = bf16[1280,1024]{1,0:T(8,128)(2,1)} async-done(((bf16[160,1024]{1,0:T(8,128)(2,1)}), bf16[1280,1024]{1,0:T(8,128)(2,1)}) %all-gather.9.cloned.1.call-update) | async-done | bytes 2621456 | tf_op jit(solution)/shard_map/all_gather | solution.py:111
  71.6 2.1 slice.161
  78.5 1.1 convolution_convert_fusion.6
  80.0 19.5 %reduce-scatter.6.cloned.1.call-done = bf16[48,1152]{1,0:T(8,128)(2,1)} async-done(((bf16[192,1152]{1,0:T(8,128)(2,1)}), bf16[48,1152]{1,0:T(8,128)(2,1)}) %reduce-scatter.6.cloned.1.call-update) | async-done | bytes 110608 | tf_op jit(solution)/shard_map/reduce_scatter | solution.py:147
  101.1 1.2 multiply_reduce_fusion
  102.3 1.7 multiply_convert_fusion.2
  107.0 1.9 copy.61
  111.2 4.4 maximum_bitcast_fusion
  115.6 3.1 reshape.329
  118.8 61.1 %all_to_all.10 = bf16[8,144,648]{2,1,0:T(8,128)(2,1)S(1)} all-to-all(bf16[8,144,648]{2,1,0:T(8,128)(2,1)} %reshape.329), channel_id=1, replica_groups=mesh['dp'=8,'mp'=4] {'dp'}, dimensions={0} | all-to-all | bytes 2985984 | tf_op jit(solution)/shard_map/all_to_all | solution.py:124
  179.8 4.0 fusion.14
  183.8 1.5 copy-done.7
  185.8 3.3 convolution_convert_fusion
  189.9 100.5 %reduce-scatter.8.cloned.1.call-done = bf16[48,1152]{1,0:T(8,128)(2,1)} async-done(((bf16[1536,1152]{1,0:T(8,128)(2,1)}), bf16[48,1152]{1,0:T(8,128)(2,1)}) %reduce-scatter.8.cloned.1.call-update) | async-done | bytes 110608 | tf_op jit(solution)/shard_map/reduce_scatter | solution.py:169
  291.5 1.2 fusion.41
  292.6 1.7 fusion.44
  294.4 59.1 %all-gather.7.cloned.1.call-done = bf16[1536,1152]{1,0:T(8,128)(2,1)} async-done(((bf16[48,1152]{1,0:T(8,128)(2,1)}), bf16[1536,1152]{1,0:T(8,128)(2,1)}) %all-gather.7.cloned.1.call-update) | async-done | bytes 3538960 | tf_op jit(solution)/shard_map/all_gather | solution.py:173
  353.5 5.0 fusion.11
  359.3 4.2 convolution_convert_fusion.1
  363.8 101.8 %reduce-scatter.10.cloned.1.call-done = bf16[48,1152]{1,0:T(8,128)(2,1)} async-done(((bf16[1536,1152]{1,0:T(8,128)(2,1)}), bf16[48,1152]{1,0:T(8,128)(2,1)}) %reduce-scatter.10.cloned.1.call-update) | async-done | bytes 110608 | tf_op jit(solution)/shard_map/reduce_scatter | solution.py:179
  465.5 1.2 fusion.42
  466.8 2.0 fusion.39
  469.0 6.8 %all_gather.26 = bf16[192,1152]{1,0:T(8,128)(2,1)S(1)} all-gather(bf16[48,1152]{1,0:T(8,128)(2,1)S(1)} %fusion.45), channel_id=1, replica_groups=mesh['dp'=8,'mp'=4] {'mp'}, dimensions={0}, use_global_device_ids=true | all-gather | bytes 552960 | tf_op jit(solution)/shard_map/all_gather | solution.py:189
  478.3 1.5 convolution_convert_fusion.7
  480.1 1.4 convolution_convert_fusion.4
  481.9 1.8 convolution_convert_fusion.2
  483.7 1.7 pad_maximum_fusion
  485.4 2.9 copy.63
  488.3 11.8 %reduce-scatter.12.cloned.1.call-done = bf16[48,1152]{1,0:T(8,128)(2,1)} async-done(((bf16[192,1152]{1,0:T(8,128)(2,1)}), bf16[48,1152]{1,0:T(8,128)(2,1)}) %reduce-scatter.12.cloned.1.call-update) | async-done | bytes 110608 | tf_op jit(solution)/shard_map/reduce_scatter | solution.py:208
  500.0 1.2 fusion.43
  501.5 1.8 fusion.1
  503.4 3.1 convolution_convert_fusion.5
  506.7 4.1 convolution_convert_fusion.3
  512.1 61.5 %all_to_all.11 = bf16[8,144,648]{2,1,0:T(8,128)(2,1)S(1)} all-to-all(bf16[8,144,648]{2,1,0:T(8,128)(2,1)S(1)} %pad_maximum_fusion.1), channel_id=1, replica_groups=mesh['dp'=8,'mp'=4] {'dp'}, dimensions={0} | all-to-all | bytes 2985984 | tf_op jit(solution)/shard_map/all_to_all | solution.py:183
  573.6 4.9 reshape.342
  578.4 8.8 %fusion.116 = (f32[1,144,8,216]{3,0,1,2:T(1,128)S(1)}, f32[1,144,8,216]{3,0,1,2:T(1,128)S(1)}, f32[1,144,8,216]{3,0,1,2:T(1,128)S(1)}) fusion(f32[3,144,8,216]{3,0,1,2:T(4,128)} %bitcast.45), kind=kLoop, calls=%fused_computation.220 | loop fusion | bytes 5971968 | tf_op jit(solution)/shard_map/slice | solution.py:246
  587.9 1.4 squeeze.17
  590.0 1.4 squeeze.16
  592.2 1.4 squeeze.15
  593.6 6.7 %all_gather.24 = bf16[192,1152]{1,0:T(8,128)(2,1)S(1)} all-gather(bf16[48,1152]{1,0:T(8,128)(2,1)S(1)} %copy-done.18), channel_id=1, replica_groups=mesh['dp'=8,'mp'=4] {'mp'}, dimensions={0}, use_global_device_ids=true | all-gather | bytes 552960 | tf_op jit(solution)/shard_map/all_gather | solution.py:235
  601.4 6.8 %all_gather.27 = bf16[192,1152]{1,0:T(8,128)(2,1)S(1)} all-gather(bf16[48,1152]{1,0:T(8,128)(2,1)S(1)} %fusion.47), channel_id=1, replica_groups=mesh['dp'=8,'mp'=4] {'mp'}, dimensions={0}, use_global_device_ids=true | all-gather | bytes 552960 | tf_op jit(solution)/shard_map/all_gather | solution.py:236
  609.2 1.0 bitcast_convert_fusion
  611.9 29.4 %all-reduce.10.cloned.1.call-done = f32[74368]{0:T(1024)} async-done(((f32[74368]{0:T(1024)}), f32[74368]{0:T(1024)}) %all-reduce.10.cloned.1.call-update) | async-done | bytes 297488 | tf_op jit(solution)/shard_map/psum | solution.py:232
  643.1 1.3 fusion.117
  644.4 1.5 fusion.118
  (247 shorter events, 30.7 us)
Async XLA Ops:
  7.2 63.4 %all-gather.9.cloned.1.call-start = ((), (), s32[]{:S(2)}) async-start(), calls=%async_computation.15 | async-start | bytes 2949120 | tf_op jit(solution)/shard_map/all_gather | solution.py:111
  13.1 86.4 %reduce-scatter.6.cloned.1.call-start = ((), (), s32[]{:S(2)}) async-start(), calls=%async_computation.7 | async-start | bytes 552960 | tf_op jit(solution)/shard_map/reduce_scatter | solution.py:147
  15.0 60.9 %copy-start.57 = (f32[128]{0:T(128)}, f32[128]{0:T(128)S(1)}, u32[]{:S(2)}) copy-start(f32[128]{0:T(128)S(1)} %multiply_power_fusion) | copy-start | bytes 1540
  16.2 58.7 %copy-start.59 = (f32[192]{0:T(256)}, f32[192]{0:T(256)S(1)}, u32[]{:S(2)}) copy-start(f32[192]{0:T(256)S(1)} %add_rsqrt_fusion) | copy-start | bytes 2308
  16.2 59.7 %copy-start.45 = (f32[192]{0:T(256)}, f32[192]{0:T(256)S(1)}, u32[]{:S(2)}) copy-start(f32[192]{0:T(256)S(1)} %fusion.98) | copy-start | bytes 2308
  71.5 3.3 copy-start.6
  73.6 3.9 copy-start.4
  75.5 2.1 copy-start.1
  77.0 27.1 %copy-start.14 = (bf16[144,1728]{1,0:T(8,128)(2,1)S(1)}, bf16[144,1728]{1,0:T(8,128)(2,1)}, u32[]{:S(2)}) copy-start(bf16[144,1728]{1,0:T(8,128)(2,1)} %param.23) | copy-start | bytes 1492996
  79.7 100.1 %all-gather.5.cloned.1.call-start = ((), (), s32[]{:S(2)}) async-start(), calls=%async_computation.8 | async-start | bytes 3649536 | tf_op jit(solution)/shard_map/all_gather | solution.py:158
  79.8 25.3 %copy-start.33 = (f32[48]{0:T(128)}, f32[48]{0:T(128)S(1)}, u32[]{:S(2)}) copy-start(f32[48]{0:T(128)S(1)} %dynamic_slice.10) | copy-start | bytes 580
  101.1 4.0 copy-start.43
  101.1 4.9 copy-start.15
  102.3 2.8 copy-start.65
  102.3 2.8 copy-start.51
  104.1 186.4 %reduce-scatter.8.cloned.1.call-start = ((), (), s32[]{:S(2)}) async-start(), calls=%async_computation.9 | async-start | bytes 3649536 | tf_op jit(solution)/shard_map/reduce_scatter | solution.py:169
  106.0 2.9 copy-start.16
  183.8 1.5 copy-start.7
  189.1 102.3 %copy-start.21 = (bf16[192,1152]{1,0:T(8,128)(2,1)S(1)}, bf16[192,1152]{1,0:T(8,128)(2,1)}, u32[]{:S(2)}) copy-start(bf16[192,1152]{1,0:T(8,128)(2,1)} %param.18) | copy-start | bytes 1327108
  189.1 102.3 %copy-start.34 = (f32[48]{0:T(128)S(1)}, f32[48]{0:T(128)}, u32[]{:S(2)}) copy-start(f32[48]{0:T(128)} %copy-done.33) | copy-start | bytes 580
  189.1 164.3 %all-gather.7.cloned.1.call-start = ((), (), s32[]{:S(2)}) async-start(), calls=%async_computation.10 | async-start | bytes 3649536 | tf_op jit(solution)/shard_map/all_gather | solution.py:173
  294.4 171.2 %reduce-scatter.10.cloned.1.call-start = ((), (), s32[]{:S(2)}) async-start(), calls=%async_computation.11 | async-start | bytes 3649536 | tf_op jit(solution)/shard_map/reduce_scatter | solution.py:179
  358.5 5.0 copy-start.68
  363.5 102.0 %copy-start.3 = (bf16[48,1152]{1,0:T(8,128)(2,1)S(1)}, bf16[48,1152]{1,0:T(8,128)(2,1)}, u32[]{:S(2)}) copy-start(bf16[48,1152]{1,0:T(8,128)(2,1)} %reduce-scatter.6.cloned.1.call-done) | copy-start | bytes 331780
  363.5 102.0 %copy-start.44 = (f32[48]{0:T(128)S(1)}, f32[48]{0:T(128)}, u32[]{:S(2)}) copy-start(f32[48]{0:T(128)} %copy-done.43) | copy-start | bytes 580
  363.5 102.0 %copy-start.52 = (f32[48]{0:T(128)S(1)}, f32[48]{0:T(128)}, u32[]{:S(2)}) copy-start(f32[48]{0:T(128)} %copy-done.51) | copy-start | bytes 580
  363.5 103.3 %copy-start.66 = (f32[48]{0:T(128)S(1)}, f32[48]{0:T(128)}, u32[]{:S(2)}) copy-start(f32[48]{0:T(128)} %copy-done.65) | copy-start | bytes 580
  363.5 103.3 %copy-start.11 = (bf16[48,1152]{1,0:T(8,128)(2,1)S(1)}, bf16[48,1152]{1,0:T(8,128)(2,1)}, u32[]{:S(2)}) copy-start(bf16[48,1152]{1,0:T(8,128)(2,1)} %reduce-scatter.8.cloned.1.call-done) | copy-start | bytes 331780
  363.6 105.3 %copy-start.64 = (f32[48]{0:T(128)S(1)}, f32[48]{0:T(128)}, u32[]{:S(2)}) copy-start(f32[48]{0:T(128)} %copy-done.63) | copy-start | bytes 580
  363.6 112.3 %copy-start.5 = (bf16[8,144,1024]{2,1,0:T(8,128)(2,1)S(1)}, bf16[8,144,1024]{2,1,0:T(8,128)(2,1)}, u32[]{:S(2)}) copy-start(bf16[8,144,1024]{2,1,0:T(8,128)(2,1)} %copy-done.4) | copy-start | bytes 7077892
  363.6 136.5 %reduce-scatter.12.cloned.1.call-start = ((), (), s32[]{:S(2)}) async-start(), calls=%async_computation.12 | async-start | bytes 552960 | tf_op jit(solution)/shard_map/reduce_scatter | solution.py:208
  363.7 112.5 %copy-start.13 = (f32[192,192]{0,1:T(8,128)S(1)}, f32[192,192]{0,1:T(8,128)}, u32[]{:S(2)}) copy-start(f32[192,192]{0,1:T(8,128)} %copy-done.12) | copy-start | bytes 442372
  363.7 112.5 %copy-start.54 = (f32[192]{0:T(256)S(1)}, f32[192]{0:T(256)}, u32[]{:S(2)}) copy-start(f32[192]{0:T(256)} %copy-done.53) | copy-start | bytes 2308
  363.8 112.5 %copy-start.56 = (f32[192]{0:T(256)S(1)}, f32[192]{0:T(256)}, u32[]{:S(2)}) copy-start(f32[192]{0:T(256)} %copy-done.55) | copy-start | bytes 2308
  466.8 21.5 %copy-start.61 = (f32[48]{0:T(128)}, f32[48]{0:T(128)S(1)}, u32[]{:S(2)}) copy-start(f32[48]{0:T(128)S(1)} %get-tuple-element.29) | copy-start | bytes 580
  468.9 7.9 %copy-start.8 = (f32[48,1152]{1,0:T(8,128)}, f32[48,1152]{1,0:T(8,128)S(1)}, u32[]{:S(2)}) copy-start(f32[48,1152]{1,0:T(8,128)S(1)} %get-tuple-element.34) | copy-start | bytes 663556
  468.9 7.6 %copy-start.2 = (f32[192,768]{1,0:T(8,128)S(1)}, f32[192,768]{1,0:T(8,128)}, u32[]{:S(2)}) copy-start(f32[192,768]{1,0:T(8,128)} %copy-done.1) | copy-start | bytes 1769476
  476.5 1.8 copy-start.67
  478.3 1.8 copy-start.20
  478.3 3.6 copy-start.31
  478.3 3.6 copy-start.60
  479.9 129.4 %reduce-scatter.14.cloned.1.call-start = ((), (), s32[]{:S(2)}) async-start(), calls=%async_computation.13 | async-start | bytes 2949120 | tf_op jit(solution)/shard_map/reduce_scatter | solution.py:225
  503.3 3.4 copy-start.69
  503.3 138.0 %all-reduce.10.cloned.1.call-start = ((), (), s32[]{:S(2)}) async-start(), calls=%async_computation.14 | async-start | bytes 598016 | tf_op jit(solution)/shard_map/psum | solution.py:232
  591.5 2.2 copy-start.18
  592.2 8.2 %copy-start.62 = (f32[48]{0:T(128)S(1)}, f32[48]{0:T(128)}, u32[]{:S(2)}) copy-start(f32[48]{0:T(128)} %copy-done.61) | copy-start | bytes 580
  592.2 8.2 %copy-start.9 = (f32[48,1152]{1,0:T(8,128)S(1)}, f32[48,1152]{1,0:T(8,128)}, u32[]{:S(2)}) copy-start(f32[48,1152]{1,0:T(8,128)} %copy-done.8) | copy-start | bytes 663556
  592.2 8.2 %copy-start.17 = (bf16[48,1152]{1,0:T(8,128)(2,1)S(1)}, bf16[48,1152]{1,0:T(8,128)(2,1)}, u32[]{:S(2)}) copy-start(bf16[48,1152]{1,0:T(8,128)(2,1)} %reduce-scatter.12.cloned.1.call-done) | copy-start | bytes 331780
  (32 other events, 31.8 us)
Sparse Core Ops, SparseCore 0:
  13.2 57.3 all-gather.8
  79.8 19.6 reduce-scatter.5
  104.2 70.9 all-gather.4
  189.3 101.1 reduce-scatter.7
  294.5 58.9 all-gather.6
  363.7 101.7 reduce-scatter.9
  480.0 20.0 reduce-scatter.11
  503.6 93.4 reduce-scatter.13
  611.3 29.9 all-reduce.9
where the time goes:
time: 654 us; the launch traced here: 653 us
  waiting for transfers between devices  377 us (58%)
  blocking collectives  143 us (22%)
  local copies, waits for them, and re-layouts  54 us (8%)
  other arithmetic  32.3 us (5%)
  matrix products  31.6 us (5%)
  between operations  15.1 us (2%)
    reduce_scatter x1, waiting for transfers between devices, on_device(): lax.psum_scatter(d_mid_part, ('dp', 'mp'), scatter_dimension=0, tiled=True)  102 us
    reduce_scatter x1, waiting for transfers between devices, on_device(): lax.psum_scatter(ffn_part, ('dp', 'mp'), scatter_dimension=0, tiled=True)  101 us
    all_to_all x1, blocking collectives, on_device(): lax.all_to_all(ffn_grad, 'dp', split_axis=0, concat_axis=0, tiled=True)  61.5 us
    all_to_all x1, blocking collectives, on_device(): lax.all_to_all(ffn_block, 'dp', split_axis=0, concat_axis=0, tiled=True)  61.1 us
    all_gather x1, waiting for transfers between devices, on_device(): lax.all_gather(d_ffn_own.astype(low), ('dp', 'mp'), axis=0, tiled=True)  59.1 us
    all_gather x1, waiting for transfers between devices, on_device(): packed = lax.all_gather(packed, 'dp', axis=0, tiled=False)  54.4 us
    psum x1, waiting for transfers between devices, on_device(): shared = lax.psum(shared, 'mp')  29.4 us
    reduce_scatter x1, waiting for transfers between devices, on_device(): lax.psum_scatter(attn_part, 'mp', scatter_dimension=0, tiled=True)  19.5 us
  transfers between devices with their start and end apart: 9, of which 7 were waited for; matrix products, arithmetic and copies ran while one was open for 9% of the time, Pallas kernels for 0%

commit v1 on v0

--- a/solution.py
+++ b/solution.py
@@ -229,7 +229,7 @@
             owned[share, : 4 * share + 2 * gain_head],
         ]
     )
-    shared = lax.psum(shared, "mp")
+    shared = jnp.sum(lax.all_gather(shared, "mp"), axis=0)
     kv_grad = shared[: 2 * share * head_width].reshape(share, 2 * head_width)
     gain_out = shared[2 * share * head_width :]
     mixed = lax.all_gather(mixed_own, "mp", axis=0, tiled=True)

time: 654 us -> 654 us (level); the launches traced: 653 us -> 645 us
  waiting for transfers between devices: 377 us -> 366 us
    psum x1 -> x0, waiting for transfers between devices: 29.4 us -> none  [on_device(): shared = lax.psum(shared, 'mp')]
    reduce_scatter x1, waiting for transfers between devices: 0.01 us -> 18.8 us  [on_device(): lax.psum_scatter(owned, 'dp', scatter_dimension=0, tiled=True)[0]]
where the time goes in v1:
time: 654 us; the launch traced here: 645 us
  waiting for transfers between devices  366 us (56%)
  blocking collectives  143 us (22%)
  local copies, waits for them, and re-layouts  54.2 us (8%)
  other arithmetic  34 us (5%)
  matrix products  31.6 us (5%)
  between operations  15.5 us (2%)
    reduce_scatter x1, waiting for transfers between devices, on_device(): lax.psum_scatter(d_mid_part, ('dp', 'mp'), scatter_dimension=0, tiled=True)  102 us
    reduce_scatter x1, waiting for transfers between devices, on_device(): lax.psum_scatter(ffn_part, ('dp', 'mp'), scatter_dimension=0, tiled=True)  100 us
    all_to_all x1, blocking collectives, on_device(): lax.all_to_all(ffn_grad, 'dp', split_axis=0, concat_axis=0, tiled=True)  61.5 us
    all_to_all x1, blocking collectives, on_device(): lax.all_to_all(ffn_block, 'dp', split_axis=0, concat_axis=0, tiled=True)  61.2 us
    all_gather x1, waiting for transfers between devices, on_device(): lax.all_gather(d_ffn_own.astype(low), ('dp', 'mp'), axis=0, tiled=True)  59.2 us
    all_gather x1, waiting for transfers between devices, on_device(): packed = lax.all_gather(packed, 'dp', axis=0, tiled=False)  54.4 us
    reduce_scatter x1, waiting for transfers between devices, on_device(): lax.psum_scatter(attn_part, 'mp', scatter_dimension=0, tiled=True)  19.5 us
    reduce_scatter x1, waiting for transfers between devices, on_device(): lax.psum_scatter(owned, 'dp', scatter_dimension=0, tiled=True)[0]  18.8 us
  transfers between devices with their start and end apart: 9, of which 7 were waited for; matrix products, arithmetic and copies ran while one was open for 9% of the time, Pallas kernels for 0%

profile of v1, /device:TPU:0, one launch (start us, length us, event | category | flops | bytes accessed | tf_op | source)
XLA Modules:
  0.0 644.9 jit_solution(16953379042739848265)
XLA Ops:
  7.2 4.1 concatenate.49
  11.3 1.8 fusion.25
  15.0 1.2 fusion.16
  16.2 54.4 %all-gather.12.cloned.1.call-done = bf16[1280,1024]{1,0:T(8,128)(2,1)} async-done(((bf16[160,1024]{1,0:T(8,128)(2,1)}), bf16[1280,1024]{1,0:T(8,128)(2,1)}) %all-gather.12.cloned.1.call-update) | async-done | bytes 2621456 | tf_op jit(solution)/shard_map/all_gather | solution.py:111
  71.6 2.1 slice.161
  78.5 1.1 convolution_convert_fusion.6
  80.0 19.5 %reduce-scatter.6.cloned.1.call-done = bf16[48,1152]{1,0:T(8,128)(2,1)} async-done(((bf16[192,1152]{1,0:T(8,128)(2,1)}), bf16[48,1152]{1,0:T(8,128)(2,1)}) %reduce-scatter.6.cloned.1.call-update) | async-done | bytes 110608 | tf_op jit(solution)/shard_map/reduce_scatter | solution.py:147
  101.1 1.2 multiply_reduce_fusion
  102.3 1.7 multiply_convert_fusion.2
  107.0 1.9 copy.71
  111.1 4.4 maximum_bitcast_fusion
  115.6 3.1 reshape.329
  118.7 61.2 %all_to_all.10 = bf16[8,144,648]{2,1,0:T(8,128)(2,1)S(1)} all-to-all(bf16[8,144,648]{2,1,0:T(8,128)(2,1)} %reshape.329), channel_id=1, replica_groups=mesh['dp'=8,'mp'=4] {'dp'}, dimensions={0} | all-to-all | bytes 2985984 | tf_op jit(solution)/shard_map/all_to_all | solution.py:124
  179.9 4.0 fusion.14
  183.9 1.5 copy-done.7
  185.9 3.3 convolution_convert_fusion
  190.0 100.2 %reduce-scatter.8.cloned.1.call-done = bf16[48,1152]{1,0:T(8,128)(2,1)} async-done(((bf16[1536,1152]{1,0:T(8,128)(2,1)}), bf16[48,1152]{1,0:T(8,128)(2,1)}) %reduce-scatter.8.cloned.1.call-update) | async-done | bytes 110608 | tf_op jit(solution)/shard_map/reduce_scatter | solution.py:169
  291.3 1.2 fusion.41
  292.4 1.7 fusion.44
  294.2 59.2 %all-gather.10.cloned.1.call-done = bf16[1536,1152]{1,0:T(8,128)(2,1)} async-done(((bf16[48,1152]{1,0:T(8,128)(2,1)}), bf16[1536,1152]{1,0:T(8,128)(2,1)}) %all-gather.10.cloned.1.call-update) | async-done | bytes 3538960 | tf_op jit(solution)/shard_map/all_gather | solution.py:173
  353.4 5.0 fusion.11
  359.2 4.2 convolution_convert_fusion.1
  363.7 101.7 %reduce-scatter.10.cloned.1.call-done = bf16[48,1152]{1,0:T(8,128)(2,1)} async-done(((bf16[1536,1152]{1,0:T(8,128)(2,1)}), bf16[48,1152]{1,0:T(8,128)(2,1)}) %reduce-scatter.10.cloned.1.call-update) | async-done | bytes 110608 | tf_op jit(solution)/shard_map/reduce_scatter | solution.py:179
  465.4 1.2 fusion.42
  466.7 2.0 fusion.39
  468.9 6.8 %all_gather.32 = bf16[192,1152]{1,0:T(8,128)(2,1)S(1)} all-gather(bf16[48,1152]{1,0:T(8,128)(2,1)S(1)} %fusion.45), channel_id=1, replica_groups=mesh['dp'=8,'mp'=4] {'mp'}, dimensions={0}, use_global_device_ids=true | all-gather | bytes 552960 | tf_op jit(solution)/shard_map/all_gather | solution.py:189
  478.1 1.5 convolution_convert_fusion.7
  479.9 1.4 convolution_convert_fusion.4
  481.7 1.8 convolution_convert_fusion.2
  483.5 1.7 pad_maximum_fusion
  485.2 2.9 copy.73
  488.1 11.8 %reduce-scatter.12.cloned.1.call-done = bf16[48,1152]{1,0:T(8,128)(2,1)} async-done(((bf16[192,1152]{1,0:T(8,128)(2,1)}), bf16[48,1152]{1,0:T(8,128)(2,1)}) %reduce-scatter.12.cloned.1.call-update) | async-done | bytes 110608 | tf_op jit(solution)/shard_map/reduce_scatter | solution.py:208
  499.9 1.2 fusion.43
  501.3 1.8 fusion.1
  503.2 3.1 convolution_convert_fusion.5
  506.6 4.1 convolution_convert_fusion.3
  512.0 61.5 %all_to_all.11 = bf16[8,144,648]{2,1,0:T(8,128)(2,1)S(1)} all-to-all(bf16[8,144,648]{2,1,0:T(8,128)(2,1)S(1)} %pad_maximum_fusion.1), channel_id=1, replica_groups=mesh['dp'=8,'mp'=4] {'dp'}, dimensions={0} | all-to-all | bytes 2985984 | tf_op jit(solution)/shard_map/all_to_all | solution.py:183
  573.5 4.9 reshape.342
  578.3 18.8 %reduce-scatter.14.cloned.1.call-done = bf16[1,160,1024]{2,1,0:T(8,128)(2,1)} async-done(((bf16[8,160,1024]{2,1,0:T(8,128)(2,1)}), bf16[1,160,1024]{2,1,0:T(8,128)(2,1)}) %reduce-scatter.14.cloned.1.call-update) | async-done | bytes 327696 | tf_op jit(solution)/shard_map/reduce_scatter | solution.py:225
  600.1 8.9 %fusion.116 = (f32[1,144,8,216]{3,0,1,2:T(1,128)S(1)}, f32[1,144,8,216]{3,0,1,2:T(1,128)S(1)}, f32[1,144,8,216]{3,0,1,2:T(1,128)S(1)}) fusion(f32[3,144,8,216]{3,0,1,2:T(4,128)} %bitcast.45), kind=kLoop, calls=%fused_computation.220 | loop fusion | bytes 5971968 | tf_op jit(solution)/shard_map/slice | solution.py:246
  609.7 1.4 squeeze.17
  611.9 1.4 squeeze.16
  614.0 1.4 squeeze.15
  615.5 6.7 %all_gather.30 = bf16[192,1152]{1,0:T(8,128)(2,1)S(1)} all-gather(bf16[48,1152]{1,0:T(8,128)(2,1)S(1)} %copy-done.19), channel_id=1, replica_groups=mesh['dp'=8,'mp'=4] {'mp'}, dimensions={0}, use_global_device_ids=true | all-gather | bytes 552960 | tf_op jit(solution)/shard_map/all_gather | solution.py:235
  622.2 1.0 fusion.47
  623.2 6.8 %all_gather.33 = bf16[192,1152]{1,0:T(8,128)(2,1)S(1)} all-gather(bf16[48,1152]{1,0:T(8,128)(2,1)S(1)} %fusion.47), channel_id=1, replica_groups=mesh['dp'=8,'mp'=4] {'mp'}, dimensions={0}, use_global_device_ids=true | all-gather | bytes 552960 | tf_op jit(solution)/shard_map/all_gather | solution.py:236
  631.0 1.7 slice_bitcast_fusion.1
  632.7 2.4 reduce_sum.272
  (251 shorter events, 31.2 us)
Async XLA Ops:
  7.2 63.4 %all-gather.12.cloned.1.call-start = ((), (), s32[]{:S(2)}) async-start(), calls=%async_computation.14 | async-start | bytes 2949120 | tf_op jit(solution)/shard_map/all_gather | solution.py:111
  13.1 86.4 %reduce-scatter.6.cloned.1.call-start = ((), (), s32[]{:S(2)}) async-start(), calls=%async_computation.7 | async-start | bytes 552960 | tf_op jit(solution)/shard_map/reduce_scatter | solution.py:147
  15.0 60.9 %copy-start.58 = (f32[128]{0:T(128)}, f32[128]{0:T(128)S(1)}, u32[]{:S(2)}) copy-start(f32[128]{0:T(128)S(1)} %multiply_power_fusion) | copy-start | bytes 1540
  16.2 58.7 %copy-start.60 = (f32[192]{0:T(256)}, f32[192]{0:T(256)S(1)}, u32[]{:S(2)}) copy-start(f32[192]{0:T(256)S(1)} %add_rsqrt_fusion) | copy-start | bytes 2308
  16.2 59.7 %copy-start.46 = (f32[192]{0:T(256)}, f32[192]{0:T(256)S(1)}, u32[]{:S(2)}) copy-start(f32[192]{0:T(256)S(1)} %fusion.98) | copy-start | bytes 2308
  71.5 3.3 copy-start.6
  73.6 3.9 copy-start.4
  75.5 2.1 copy-start.1
  77.0 27.1 %copy-start.15 = (bf16[144,1728]{1,0:T(8,128)(2,1)S(1)}, bf16[144,1728]{1,0:T(8,128)(2,1)}, u32[]{:S(2)}) copy-start(bf16[144,1728]{1,0:T(8,128)(2,1)} %param.23) | copy-start | bytes 1492996
  79.7 100.3 %all-gather.8.cloned.1.call-start = ((), (), s32[]{:S(2)}) async-start(), calls=%async_computation.8 | async-start | bytes 3649536 | tf_op jit(solution)/shard_map/all_gather | solution.py:158
  79.8 25.2 %copy-start.34 = (f32[48]{0:T(128)}, f32[48]{0:T(128)S(1)}, u32[]{:S(2)}) copy-start(f32[48]{0:T(128)S(1)} %dynamic_slice.10) | copy-start | bytes 580
  101.1 4.0 copy-start.44
  101.1 4.9 copy-start.16
  102.3 2.8 copy-start.66
  102.3 2.8 copy-start.52
  104.0 186.2 %reduce-scatter.8.cloned.1.call-start = ((), (), s32[]{:S(2)}) async-start(), calls=%async_computation.9 | async-start | bytes 3649536 | tf_op jit(solution)/shard_map/reduce_scatter | solution.py:169
  106.0 2.9 copy-start.17
  183.9 1.5 copy-start.7
  189.2 102.0 %copy-start.22 = (bf16[192,1152]{1,0:T(8,128)(2,1)S(1)}, bf16[192,1152]{1,0:T(8,128)(2,1)}, u32[]{:S(2)}) copy-start(bf16[192,1152]{1,0:T(8,128)(2,1)} %param.18) | copy-start | bytes 1327108
  189.2 102.0 %copy-start.35 = (f32[48]{0:T(128)S(1)}, f32[48]{0:T(128)}, u32[]{:S(2)}) copy-start(f32[48]{0:T(128)} %copy-done.34) | copy-start | bytes 580
  189.2 164.1 %all-gather.10.cloned.1.call-start = ((), (), s32[]{:S(2)}) async-start(), calls=%async_computation.10 | async-start | bytes 3649536 | tf_op jit(solution)/shard_map/all_gather | solution.py:173
  294.1 171.3 %reduce-scatter.10.cloned.1.call-start = ((), (), s32[]{:S(2)}) async-start(), calls=%async_computation.11 | async-start | bytes 3649536 | tf_op jit(solution)/shard_map/reduce_scatter | solution.py:179
  358.4 5.0 copy-start.69
  363.4 102.0 %copy-start.3 = (bf16[48,1152]{1,0:T(8,128)(2,1)S(1)}, bf16[48,1152]{1,0:T(8,128)(2,1)}, u32[]{:S(2)}) copy-start(bf16[48,1152]{1,0:T(8,128)(2,1)} %reduce-scatter.6.cloned.1.call-done) | copy-start | bytes 331780
  363.4 102.0 %copy-start.45 = (f32[48]{0:T(128)S(1)}, f32[48]{0:T(128)}, u32[]{:S(2)}) copy-start(f32[48]{0:T(128)} %copy-done.44) | copy-start | bytes 580
  363.4 102.0 %copy-start.53 = (f32[48]{0:T(128)S(1)}, f32[48]{0:T(128)}, u32[]{:S(2)}) copy-start(f32[48]{0:T(128)} %copy-done.52) | copy-start | bytes 580
  363.4 103.2 %copy-start.67 = (f32[48]{0:T(128)S(1)}, f32[48]{0:T(128)}, u32[]{:S(2)}) copy-start(f32[48]{0:T(128)} %copy-done.66) | copy-start | bytes 580
  363.4 103.3 %copy-start.12 = (bf16[48,1152]{1,0:T(8,128)(2,1)S(1)}, bf16[48,1152]{1,0:T(8,128)(2,1)}, u32[]{:S(2)}) copy-start(bf16[48,1152]{1,0:T(8,128)(2,1)} %reduce-scatter.8.cloned.1.call-done) | copy-start | bytes 331780
  363.4 105.3 %copy-start.65 = (f32[48]{0:T(128)S(1)}, f32[48]{0:T(128)}, u32[]{:S(2)}) copy-start(f32[48]{0:T(128)} %copy-done.64) | copy-start | bytes 580
  363.5 112.2 %copy-start.5 = (bf16[8,144,1024]{2,1,0:T(8,128)(2,1)S(1)}, bf16[8,144,1024]{2,1,0:T(8,128)(2,1)}, u32[]{:S(2)}) copy-start(bf16[8,144,1024]{2,1,0:T(8,128)(2,1)} %copy-done.4) | copy-start | bytes 7077892
  363.5 136.4 %reduce-scatter.12.cloned.1.call-start = ((), (), s32[]{:S(2)}) async-start(), calls=%async_computation.12 | async-start | bytes 552960 | tf_op jit(solution)/shard_map/reduce_scatter | solution.py:208
  363.6 112.4 %copy-start.14 = (f32[192,192]{0,1:T(8,128)S(1)}, f32[192,192]{0,1:T(8,128)}, u32[]{:S(2)}) copy-start(f32[192,192]{0,1:T(8,128)} %copy-done.13) | copy-start | bytes 442372
  363.6 112.4 %copy-start.55 = (f32[192]{0:T(256)S(1)}, f32[192]{0:T(256)}, u32[]{:S(2)}) copy-start(f32[192]{0:T(256)} %copy-done.54) | copy-start | bytes 2308
  363.7 112.4 %copy-start.57 = (f32[192]{0:T(256)S(1)}, f32[192]{0:T(256)}, u32[]{:S(2)}) copy-start(f32[192]{0:T(256)} %copy-done.56) | copy-start | bytes 2308
  466.7 21.4 %copy-start.62 = (f32[48]{0:T(128)}, f32[48]{0:T(128)S(1)}, u32[]{:S(2)}) copy-start(f32[48]{0:T(128)S(1)} %get-tuple-element.29) | copy-start | bytes 580
  468.7 7.9 %copy-start.9 = (f32[48,1152]{1,0:T(8,128)}, f32[48,1152]{1,0:T(8,128)S(1)}, u32[]{:S(2)}) copy-start(f32[48,1152]{1,0:T(8,128)S(1)} %get-tuple-element.34) | copy-start | bytes 663556
  468.7 7.6 %copy-start.2 = (f32[192,768]{1,0:T(8,128)S(1)}, f32[192,768]{1,0:T(8,128)}, u32[]{:S(2)}) copy-start(f32[192,768]{1,0:T(8,128)} %copy-done.1) | copy-start | bytes 1769476
  476.3 1.8 copy-start.68
  478.1 1.8 copy-start.21
  478.1 3.6 copy-start.32
  478.1 3.6 copy-start.61
  479.7 117.5 %reduce-scatter.14.cloned.1.call-start = ((), (), s32[]{:S(2)}) async-start(), calls=%async_computation.13 | async-start | bytes 2949120 | tf_op jit(solution)/shard_map/reduce_scatter | solution.py:225
  503.2 3.4 copy-start.70
  503.2 129.5 %all-gather.14.cloned.1.call-start = ((), (), s32[]{:S(2)}) async-start(), calls=%async_computation.15 | async-start | bytes 1487360 | tf_op jit(solution)/shard_map/all_gather | solution.py:232
  613.3 2.2 copy-start.19
  614.0 8.1 %copy-start.63 = (f32[48]{0:T(128)S(1)}, f32[48]{0:T(128)}, u32[]{:S(2)}) copy-start(f32[48]{0:T(128)} %copy-done.62) | copy-start | bytes 580
  614.0 8.1 %copy-start.10 = (f32[48,1152]{1,0:T(8,128)S(1)}, f32[48,1152]{1,0:T(8,128)}, u32[]{:S(2)}) copy-start(f32[48,1152]{1,0:T(8,128)} %copy-done.9) | copy-start | bytes 663556
  614.0 8.1 %copy-start.18 = (bf16[48,1152]{1,0:T(8,128)(2,1)S(1)}, bf16[48,1152]{1,0:T(8,128)(2,1)}, u32[]{:S(2)}) copy-start(bf16[48,1152]{1,0:T(8,128)(2,1)} %reduce-scatter.12.cloned.1.call-done) | copy-start | bytes 331780
  (33 other events, 32.6 us)
Sparse Core Ops, SparseCore 0:
  13.2 57.3 all-gather.11
  79.8 19.6 reduce-scatter.5
  104.1 71.6 all-gather.7
  189.4 100.7 reduce-scatter.7
  294.3 59.0 all-gather.9
  363.6 101.7 reduce-scatter.9
  479.8 20.1 reduce-scatter.11
  503.4 93.6 reduce-scatter.13
  600.3 16.4 all-gather.13
